TPU v7x, 32 devices: a whole 2x2x4 slice. The times are simulated.
32 devices in a mesh: groups: 2 (over y), wide: 4 (over z), narrow: 4 (over x, core).
Axes of the slice: x: 2, y: 2, z: 4, core: 2. Of those that a mesh axis runs over, the one named last changes fastest.
Arguments:
- tokens: bfloat16 [1024, 7168], P('groups', ('narrow', 'wide')), parts along dimension 0, may hold values from -6 to 6
- gate_one: bfloat16 [7168, 9216], P('narrow', 'wide'), may hold values from -0.0625 to 0.0625
- up_one: bfloat16 [7168, 9216], P('narrow', 'wide'), may hold values from -0.0625 to 0.0625
- down_one: bfloat16 [9216, 7168], P('wide', 'narrow'), may hold values from -0.09375 to 0.09375
- gate_two: bfloat16 [4, 1792, 9216], P(None, 'wide', 'narrow'), may hold values from -0.0625 to 0.0625
- up_two: bfloat16 [4, 1792, 9216], P(None, 'wide', 'narrow'), may hold values from -0.0625 to 0.0625
- down_two: bfloat16 [9216, 4, 1792], P('narrow', None, 'wide'), may hold values from -0.09375 to 0.09375
Outputs:
- result: bfloat16 [1024, 7168], P('groups', ('narrow', 'wide')), parts along dimension 0
There are 2 independent parts, one for each index of `groups`. A program takes and returns all parts, laid end to end along the dimension named above; an argument that names none is the same for every part. Nothing has to cross between parts.
All inputs are finite; a program needn't handle non-finite values.
Results may differ from a plain program's by a relative error of at most 0.03.
Values may be sent and summed in bfloat16 or wider, within the bound.
A program may use at most 128 MiB of HBM per device.

v0:
```python
import jax
import jax.numpy as jnp
from jax import lax
from jax.sharding import PartitionSpec as P


def pair_fold(first_matrix, second_matrix, piece):
    return (
        jnp.dot(piece, first_matrix, preferred_element_type=jnp.float32),
        jnp.dot(piece, second_matrix, preferred_element_type=jnp.float32),
    )


def single_fold(matrix, piece):
    return jnp.dot(piece, matrix, preferred_element_type=jnp.float32)


def swiglu(gate, up_value):
    return (jax.nn.silu(gate) * up_value).astype(jnp.bfloat16)


def per_device(tokens, gate_one, up_one, down_one, gate_two, up_two, down_two):
    gate_part, up_part = pair_fold(
        gate_one, up_one, lax.all_gather(tokens, "wide", axis=1, tiled=True)
    )
    gate_share, up_share = (
        lax.psum_scatter(
            gate_part.astype(jnp.bfloat16), "narrow", scatter_dimension=1, tiled=True
        ).astype(jnp.float32),
        lax.psum_scatter(
            up_part.astype(jnp.bfloat16), "narrow", scatter_dimension=1, tiled=True
        ).astype(jnp.float32),
    )
    hidden_share = swiglu(gate_share, up_share)
    down_part = single_fold(down_one, lax.all_gather(hidden_share, "narrow", axis=1, tiled=True))
    mixed_first = lax.psum_scatter(
        down_part.astype(jnp.bfloat16), "wide", scatter_dimension=1, tiled=True
    ).astype(jnp.float32)
    middle = (tokens.astype(jnp.float32) + mixed_first).astype(jnp.bfloat16)
    gate_flat = gate_two.reshape(-1, gate_two.shape[2])
    up_flat = up_two.reshape(-1, up_two.shape[2])
    down_flat = down_two.reshape(down_two.shape[0], -1)
    gate_part2, up_part2 = pair_fold(
        gate_flat, up_flat, lax.all_gather(middle, "narrow", axis=1, tiled=True)
    )
    gate_share2, up_share2 = (
        lax.psum_scatter(
            gate_part2.astype(jnp.bfloat16), "wide", scatter_dimension=1, tiled=True
        ).astype(jnp.float32),
        lax.psum_scatter(
            up_part2.astype(jnp.bfloat16), "wide", scatter_dimension=1, tiled=True
        ).astype(jnp.float32),
    )
    hidden_share2 = swiglu(gate_share2, up_share2)
    down_part2 = single_fold(down_flat, lax.all_gather(hidden_share2, "wide", axis=1, tiled=True))
    mixed_second = lax.psum_scatter(
        down_part2.astype(jnp.bfloat16), "narrow", scatter_dimension=1, tiled=True
    ).astype(jnp.float32)
    return (middle.astype(jnp.float32) + mixed_second).astype(jnp.bfloat16)


def solution(mesh):
    return jax.shard_map(
        per_device,
        mesh=mesh,
        in_specs=(
            P("groups", ("narrow", "wide")),
            P("narrow", "wide"),
            P("narrow", "wide"),
            P("wide", "narrow"),
            P(None, "wide", "narrow"),
            P(None, "wide", "narrow"),
            P("narrow", None, "wide"),
        ),
        out_specs=P("groups", ("narrow", "wide")),
        check_vma=False,
    )
```

profile of v0, /device:TPU:0, one launch (start us, length us, event | category | flops | bytes accessed | tf_op | source)
XLA Modules:
  0.0 437.1 jit_solution(11631780464276964852)
XLA Ops:
  6.5 0.7 all-gather.5.cloned.1.call-update
  7.3 0.0 reduce-scatter.9.cloned.1.call-start
  7.3 45.8 %all-gather.5.cloned.1.call-done = bf16[512,1792]{0,1:T(8,128)(2,1)} async-done(((bf16[512,448]{0,1:T(8,128)(2,1)}), bf16[512,1792]{0,1:T(8,128)(2,1)}) %all-gather.5.cloned.1.call-update) | async-done | bytes 1835024 | tf_op jit(solution)/shard_map/all_gather | solution.py:24
  53.1 9.8 %convolution_convert_fusion.2 = bf16[512,2304]{0,1:T(8,128)(2,1)} fusion(bf16[512,1792]{0,1:T(8,128)(2,1)} %all-gather.5.cloned.1.call-done, bf16[1792,2304]{1,0:T(8,128)(2,1)} %param.9), kind=kOutput, calls=%fused_computation.2 | convolution fusion | flops 4229038080 | bytes 12451840 | tf_op jit(solution)/shard_map/dot_general | solution.py:10
  62.9 0.0 reduce-scatter.7.cloned.1.call-start
  63.0 1.4 copy-done.2
  64.4 11.4 %convolution_convert_fusion.3 = bf16[512,2304]{0,1:T(8,128)(2,1)} fusion(bf16[512,1792]{0,1:T(8,128)(2,1)S(1)} %copy-done.2, bf16[1792,2304]{1,0:T(8,128)(2,1)} %param.8), kind=kOutput, calls=%fused_computation.3 | convolution fusion | flops 4229038080 | bytes 12451840 | tf_op jit(solution)/shard_map/dot_general | solution.py:9
  75.8 0.0 all-gather.7.cloned.1.call-start
  75.9 19.1 %reduce-scatter.9.cloned.1.call-done = bf16[512,576]{0,1:T(8,128)(2,1)} async-done(((bf16[512,2304]{0,1:T(8,128)(2,1)}), bf16[512,576]{0,1:T(8,128)(2,1)}) %reduce-scatter.9.cloned.1.call-update) | async-done | bytes 589840 | tf_op jit(solution)/shard_map/reduce_scatter | solution.py:30
  95.0 35.8 %reduce-scatter.7.cloned.1.call-done = bf16[512,576]{0,1:T(8,128)(2,1)} async-done(((bf16[512,2304]{0,1:T(8,128)(2,1)}), bf16[512,576]{0,1:T(8,128)(2,1)}) %reduce-scatter.7.cloned.1.call-update) | async-done | bytes 589840 | tf_op jit(solution)/shard_map/reduce_scatter | solution.py:27
  130.8 2.4 fusion.9
  133.3 0.2 reduce-scatter.11.cloned.1.call-start
  133.5 24.0 %all-gather.7.cloned.1.call-done = bf16[512,2304]{0,1:T(8,128)(2,1)} async-done(((bf16[512,576]{0,1:T(8,128)(2,1)}), bf16[512,2304]{0,1:T(8,128)(2,1)}) %all-gather.7.cloned.1.call-update) | async-done | bytes 2359312 | tf_op jit(solution)/shard_map/all_gather | solution.py:35
  157.5 9.8 %convolution_convert_fusion.5 = bf16[512,1792]{0,1:T(8,128)(2,1)} fusion(bf16[512,2304]{0,1:T(8,128)(2,1)} %all-gather.7.cloned.1.call-done, bf16[2304,1792]{1,0:T(8,128)(2,1)} %param.10), kind=kOutput, calls=%fused_computation.5 | convolution fusion | flops 4228775936 | bytes 12451840 | tf_op jit(solution)/shard_map/dot_general | solution.py:15
  167.3 0.0 all-gather.9.cloned.1.call-start
  167.4 39.5 %reduce-scatter.11.cloned.1.call-done = bf16[512,448]{0,1:T(8,128)(2,1)} async-done(((bf16[512,1792]{0,1:T(8,128)(2,1)}), bf16[512,448]{0,1:T(8,128)(2,1)}) %reduce-scatter.11.cloned.1.call-update) | async-done | bytes 458768 | tf_op jit(solution)/shard_map/reduce_scatter | solution.py:36
  206.9 1.9 add_convert_fusion.1
  208.8 0.0 reduce-scatter.15.cloned.1.call-start
  208.9 20.4 %all-gather.9.cloned.1.call-done = bf16[512,1792]{0,1:T(8,128)(2,1)} async-done(((bf16[512,448]{0,1:T(8,128)(2,1)}), bf16[512,1792]{0,1:T(8,128)(2,1)}) %all-gather.9.cloned.1.call-update) | async-done | bytes 1835024 | tf_op jit(solution)/shard_map/all_gather | solution.py:44
  229.2 9.8 %convolution_convert_fusion = bf16[512,2304]{0,1:T(8,128)(2,1)} fusion(bf16[512,1792]{0,1:T(8,128)(2,1)} %all-gather.9.cloned.1.call-done, bf16[1792,2304]{1,0:T(8,128)(2,1)} %bitcast.15), kind=kOutput, calls=%fused_computation | convolution fusion | flops 4229038080 | bytes 12451840 | tf_op jit(solution)/shard_map/dot_general | solution.py:10
  239.1 0.3 reduce-scatter.13.cloned.1.call-start
  239.3 1.2 copy-done.3
  240.5 11.1 %convolution_convert_fusion.1 = bf16[512,2304]{0,1:T(8,128)(2,1)} fusion(bf16[512,1792]{0,1:T(8,128)(2,1)S(1)} %copy-done.3, bf16[1792,2304]{1,0:T(8,128)(2,1)} %bitcast.16), kind=kOutput, calls=%fused_computation.1 | convolution fusion | flops 4229038080 | bytes 12451840 | tf_op jit(solution)/shard_map/dot_general | solution.py:9
  251.6 0.0 all-gather.11.cloned.1.call-start
  251.7 35.6 %reduce-scatter.15.cloned.1.call-done = bf16[512,576]{0,1:T(8,128)(2,1)} async-done(((bf16[512,2304]{0,1:T(8,128)(2,1)}), bf16[512,576]{0,1:T(8,128)(2,1)}) %reduce-scatter.15.cloned.1.call-update) | async-done | bytes 589840 | tf_op jit(solution)/shard_map/reduce_scatter | solution.py:50
  287.3 49.9 %reduce-scatter.13.cloned.1.call-done = bf16[512,576]{0,1:T(8,128)(2,1)} async-done(((bf16[512,2304]{0,1:T(8,128)(2,1)}), bf16[512,576]{0,1:T(8,128)(2,1)}) %reduce-scatter.13.cloned.1.call-update) | async-done | bytes 589840 | tf_op jit(solution)/shard_map/reduce_scatter | solution.py:47
  337.1 2.4 fusion.8
  339.6 0.0 reduce-scatter.17.cloned.1.call-start
  339.6 50.1 %all-gather.11.cloned.1.call-done = bf16[512,2304]{0,1:T(8,128)(2,1)} async-done(((bf16[512,576]{0,1:T(8,128)(2,1)}), bf16[512,2304]{0,1:T(8,128)(2,1)}) %all-gather.11.cloned.1.call-update) | async-done | bytes 2359312 | tf_op jit(solution)/shard_map/all_gather | solution.py:55
  389.7 9.8 %convolution_convert_fusion.4 = bf16[512,1792]{0,1:T(8,128)(2,1)} fusion(bf16[2304,1792]{0,1:T(8,128)(2,1)} %bitcast.17, bf16[512,2304]{0,1:T(8,128)(2,1)} %all-gather.11.cloned.1.call-done), kind=kOutput, calls=%fused_computation.4 | convolution fusion | flops 4228775936 | bytes 12451840 | tf_op jit(solution)/shard_map/dot_general | solution.py:15
  399.5 28.8 %reduce-scatter.17.cloned.1.call-done = bf16[512,448]{0,1:T(8,128)(2,1)} async-done(((bf16[512,1792]{0,1:T(8,128)(2,1)}), bf16[512,448]{0,1:T(8,128)(2,1)}) %reduce-scatter.17.cloned.1.call-update) | async-done | bytes 458768 | tf_op jit(solution)/shard_map/reduce_scatter | solution.py:56
  428.3 1.9 add_convert_fusion
  (16 shorter events, 0.2 us)
Async XLA Ops:
  6.5 46.5 %all-gather.5.cloned.1.call-start = ((), (), s32[]{:S(2)}) async-start(), calls=%async_computation.6 | async-start | bytes 2293760 | tf_op jit(solution)/shard_map/all_gather | solution.py:24
  7.3 87.7 %reduce-scatter.9.cloned.1.call-start = ((), (), s32[]{:S(2)}) async-start(), calls=%async_computation.8 | async-start | bytes 2949120 | tf_op jit(solution)/shard_map/reduce_scatter | solution.py:30
  62.9 1.5 copy-start.2
  62.9 67.9 %reduce-scatter.7.cloned.1.call-start = ((), (), s32[]{:S(2)}) async-start(), calls=%async_computation.7 | async-start | bytes 2949120 | tf_op jit(solution)/shard_map/reduce_scatter | solution.py:27
  75.8 81.6 %all-gather.7.cloned.1.call-start = ((), (), s32[]{:S(2)}) async-start(), calls=%async_computation.9 | async-start | bytes 2949120 | tf_op jit(solution)/shard_map/all_gather | solution.py:35
  133.2 73.6 %copy-start.1 = (bf16[512,448]{0,1:T(8,128)(2,1)S(1)}, bf16[512,448]{0,1:T(8,128)(2,1)}, u32[]{:S(2)}) copy-start(bf16[512,448]{0,1:T(8,128)(2,1)} %param.7) | copy-start | bytes 1376260
  133.3 73.6 %reduce-scatter.11.cloned.1.call-start = ((), (), s32[]{:S(2)}) async-start(), calls=%async_computation.10 | async-start | bytes 2293760 | tf_op jit(solution)/shard_map/reduce_scatter | solution.py:36
  167.3 61.9 %all-gather.9.cloned.1.call-start = ((), (), s32[]{:S(2)}) async-start(), calls=%async_computation.11 | async-start | bytes 2293760 | tf_op jit(solution)/shard_map/all_gather | solution.py:44
  208.8 78.5 %reduce-scatter.15.cloned.1.call-start = ((), (), s32[]{:S(2)}) async-start(), calls=%async_computation.13 | async-start | bytes 2949120 | tf_op jit(solution)/shard_map/reduce_scatter | solution.py:50
  239.0 1.5 copy-start.3
  239.1 98.1 %reduce-scatter.13.cloned.1.call-start = ((), (), s32[]{:S(2)}) async-start(), calls=%async_computation.12 | async-start | bytes 2949120 | tf_op jit(solution)/shard_map/reduce_scatter | solution.py:47
  251.6 138.1 %all-gather.11.cloned.1.call-start = ((), (), s32[]{:S(2)}) async-start(), calls=%async_computation.14 | async-start | bytes 2949120 | tf_op jit(solution)/shard_map/all_gather | solution.py:55
  339.6 88.7 %reduce-scatter.17.cloned.1.call-start = ((), (), s32[]{:S(2)}) async-start(), calls=%async_computation.15 | async-start | bytes 2293760 | tf_op jit(solution)/shard_map/reduce_scatter | solution.py:56
  389.7 38.6 %copy-start = (bf16[512,448]{0,1:T(8,128)(2,1)S(1)}, bf16[512,448]{0,1:T(8,128)(2,1)}, u32[]{:S(2)}) copy-start(bf16[512,448]{0,1:T(8,128)(2,1)} %add_convert_fusion.1) | copy-start | bytes 1376260
Sparse Core Ops, SparseCore 0:
  8.9 44.0 all-gather.4
  63.0 31.9 reduce-scatter.8
  97.7 33.0 reduce-scatter.6
  133.4 24.0 all-gather.6
  167.4 39.4 reduce-scatter.10
  208.9 20.2 all-gather.8
  239.2 48.0 reduce-scatter.14
  289.6 47.5 reduce-scatter.12
  339.7 49.9 all-gather.10
  399.6 28.6 reduce-scatter.16
where the time goes:
time: 437 us
  waiting for transfers between devices  350 us (80%)
  matrix products  61.7 us (14%)
  between operations  13.5 us (3%)
  other arithmetic  8.67 us (2%)
    all_gather x1, waiting for transfers between devices, per_device(): lax.all_gather(hidden_share2, 'wide', axis=1, tiled=True)  50.1 us
    reduce_scatter x1, waiting for transfers between devices, per_device(): lax.psum_scatter(gate_part2.astype(jnp.bfloat16), 'wide', scatter_dimensi...  49.9 us
    all_gather x1, waiting for transfers between devices, per_device(): lax.all_gather(tokens, 'wide', axis=1, tiled=True)  45.8 us
    reduce_scatter x1, waiting for transfers between devices, per_device(): lax.psum_scatter(down_part.astype(jnp.bfloat16), 'wide', scatter_dimensio...  39.5 us
    reduce_scatter x1, waiting for transfers between devices, per_device(): lax.psum_scatter(gate_part.astype(jnp.bfloat16), 'narrow', scatter_dimens...  35.8 us
    reduce_scatter x1, waiting for transfers between devices, per_device(): lax.psum_scatter(up_part2.astype(jnp.bfloat16), 'wide', scatter_dimension...  35.6 us
    reduce_scatter x1, waiting for transfers between devices, per_device(): lax.psum_scatter(down_part2.astype(jnp.bfloat16), 'narrow', scatter_dimen...  28.8 us
    all_gather x1, waiting for transfers between devices, per_device(): lax.all_gather(hidden_share, 'narrow', axis=1, tiled=True)  24 us
  transfers between devices with their start and end apart: 10, of which 10 were waited for; matrix products, arithmetic and copies ran while one was open for 5% of the time, Pallas kernels for 0%

commit v1 on v0

v1 whole, which is shorter than its diff:
```python
import functools

import jax
import jax.numpy as jnp
from jax import lax
from jax.experimental import pallas as pl
from jax.experimental.pallas import tpu as pltpu
from jax.sharding import PartitionSpec as P

BF = jnp.bfloat16
F32 = jnp.float32
LINE = 4
MIB = 1024 * 1024
LAG = 2


def swiglu(gate, up_value):
    return (jax.nn.silu(gate) * up_value).astype(BF)


def plain(tokens, gate_one, up_one, down_one, gate_two, up_two, down_two):
    def layer(entries, gate, up, down, gather, scatter):
        whole = lax.all_gather(entries, gather, axis=1, tiled=True)
        shares = [
            lax.psum_scatter(
                jnp.dot(whole, w, preferred_element_type=F32).astype(BF),
                scatter, scatter_dimension=1, tiled=True,
            ).astype(F32)
            for w in (gate, up)
        ]
        hidden = lax.all_gather(swiglu(*shares), scatter, axis=1, tiled=True)
        part = jnp.dot(hidden, down, preferred_element_type=F32).astype(BF)
        mixed = lax.psum_scatter(part, gather, scatter_dimension=1, tiled=True)
        return (entries.astype(F32) + mixed.astype(F32)).astype(BF)

    middle = layer(tokens, gate_one, up_one, down_one, "wide", "narrow")
    return layer(
        middle,
        gate_two.reshape(-1, gate_two.shape[2]),
        up_two.reshape(-1, up_two.shape[2]),
        down_two.reshape(down_two.shape[0], -1),
        "narrow", "wide",
    )


def kernel(
    tok, g1, u1, d1, g2, u2, d2, out,
    wgu, wd, tokens, part, near, across, hid1, dpart, zr, zl, mid, yr, yl, hid2,
    near8, across8, acc_gu, acc_h, wsem, tsem, send_sems, recv_sems,
):
    z = lax.axis_index("wide")
    n = lax.axis_index("narrow")
    core = lax.rem(n, 2)
    chip = n // 2
    twin = chip * 2 + (1 - core)
    peer = (1 - chip) * 2 + core
    far = (1 - chip) * 2 + (1 - core)
    halves, rows = tokens.shape[0], tokens.shape[2]
    quarter = rows // LINE
    depth = tokens.shape[3]
    units = hid1.shape[2]

    def load(slot, src, dst):
        copy = pltpu.make_async_copy(src, dst, wsem.at[slot])
        copy.start()
        return copy

    own_rows = [
        pltpu.make_async_copy(tok.at[pl.ds(m * rows, rows)], tokens.at[m, z], tsem.at[m])
        for m in range(halves)
    ]
    for copy in own_rows:
        copy.start()
    loads = {
        "gu1": [load(0, g1, wgu.at[0]), load(1, u1, wgu.at[1])],
        "d1": [load(2, d1, wd)],
    }

    barrier = pltpu.get_barrier_semaphore()
    pl.semaphore_signal(barrier, inc=1, device_id={"narrow": twin})
    pl.semaphore_signal(barrier, inc=1, device_id={"narrow": peer})

    @pl.when(z > 0)
    def _():
        pl.semaphore_signal(barrier, inc=1, device_id={"wide": z - 1})

    @pl.when(z < LINE - 1)
    def _():
        pl.semaphore_signal(barrier, inc=1, device_id={"wide": z + 1})

    inner = jnp.logical_and(z > 0, z < LINE - 1)

    @pl.when(inner)
    def _():
        pl.semaphore_wait(barrier, 4)

    @pl.when(jnp.logical_not(inner))
    def _():
        pl.semaphore_wait(barrier, 3)

    counter = [0]

    def message(src, dst, device):
        i = counter[0]
        counter[0] += 1
        return pltpu.make_async_remote_copy(
            src_ref=src, dst_ref=dst, send_sem=send_sems.at[i], recv_sem=recv_sems.at[i],
            device_id=device, device_id_type=pl.DeviceIdType.MESH,
        )

    pending = [[] for _ in range(halves)]

    def guarded(cond, f):
        if cond is None:
            f()
        else:
            pl.when(cond)(f)

    def start(m, copy, cond=None):
        guarded(cond, copy.start)
        pending[m].append((cond, copy.wait_send))

    def arrive(copy, cond=None):
        guarded(cond, copy.wait_recv)

    def flush(m):
        for cond, wait in pending[m]:
            guarded(cond, wait)
        pending[m].clear()

    def piece(i):
        return pl.ds(pl.multiple_of(i * quarter, quarter), quarter)

    right, left = {"wide": z + 1}, {"wide": z - 1}

    def gather_line(m, at):
        previous = None
        for step in range(1, LINE):
            if previous is not None:
                yield
                arrive(previous[0], z >= step - 1)
                arrive(previous[1], z <= LINE - step)
            own = step - 1
            to_right = message(at(lax.max(z - own, 0)), at(lax.max(z - own, 0)), right)
            to_left = message(at(lax.min(z + own, LINE - 1)), at(lax.min(z + own, LINE - 1)), left)
            start(m, to_right, jnp.logical_and(z >= own, z < LINE - 1))
            start(m, to_left, jnp.logical_and(z + own < LINE, z > 0))
            previous = (to_right, to_left)
        yield
        arrive(previous[0], z >= LINE - 1)
        arrive(previous[1], z <= 0)

    def scatter_line(m, at, from_left, from_right):
        back = LINE - 1 - z
        previous = None

        def add(index, ref, slot):
            dst = at(index)
            dst[...] = (dst[...].astype(F32) + ref[slot].astype(F32)).astype(BF)

        for step in range(1, LINE):
            goes_right = jnp.logical_and(z <= step - 1, z < LINE - 1)
            goes_left = jnp.logical_and(back <= step - 1, back < LINE - 1)
            to_r = lax.min(z + LINE - step, LINE - 1)
            to_l = LINE - 1 - lax.min(back + LINE - step, LINE - 1)
            if previous is not None:
                yield
                arrive(previous[0], jnp.logical_and(z >= 1, z <= step - 1))
                arrive(previous[1], jnp.logical_and(back >= 1, back <= step - 1))

                @pl.when(jnp.logical_and(goes_right, z >= 1))
                def _():
                    add(to_r, from_left, step - 2)

            to_right = message(at(to_r), from_left.at[step - 1], right)
            start(m, to_right, goes_right)
            if previous is not None:
                @pl.when(jnp.logical_and(goes_left, back >= 1))
                def _():
                    add(to_l, from_right, step - 2)

            to_left = message(at(to_l), from_right.at[step - 1], left)
            start(m, to_left, goes_left)
            previous = (to_right, to_left)
        yield
        arrive(previous[0], z >= 1)
        arrive(previous[1], back >= 1)

    def gather_narrow(m, at):
        a = message(at(n), at(n), {"narrow": peer})
        b = message(at(n), at(n), {"narrow": twin})
        start(m, a)
        start(m, b)
        yield
        arrive(a)
        c = message(at(peer), at(peer), {"narrow": twin})
        start(m, c)
        yield
        arrive(b)
        arrive(c)

    def scatter_narrow(m, at, two, one):
        copies = []
        for i in range(2):
            copies.append(message(at(i * 2 + (1 - core)), two.at[i], {"narrow": twin}))
            start(m, copies[-1])
        yield
        for copy in copies:
            arrive(copy)
        dst = at(peer)
        dst[...] = (dst[...].astype(F32) + two[1 - chip].astype(F32)).astype(BF)
        over = message(at(peer), one, {"narrow": peer})
        start(m, over)
        yield
        arrive(over)

    def gate_up(m, src):
        tile = 256

        def body(i, carry):
            c = pl.ds(pl.multiple_of(i * tile, tile), tile)
            for w in range(2):
                total = jnp.dot(src[m, 0], wgu[w, 0:depth, c], preferred_element_type=F32)
                for s in range(1, LINE):
                    total += jnp.dot(
                        src[m, s], wgu[w, s * depth:(s + 1) * depth, c], preferred_element_type=F32
                    )
                dst = pl.ds(pl.multiple_of(w * units + i * tile, tile), tile)
                part[m, :, dst] = total.astype(BF)
            return carry

        lax.fori_loop(0, units // tile, body, 0)

    def down(m, hidden):
        for g in range(2):
            total = jnp.dot(
                hidden[m], wd[:, g * 2 * depth:(g + 1) * 2 * depth], preferred_element_type=F32
            )
            dpart[m, 2 * g] = total[:, :depth].astype(BF)
            dpart[m, 2 * g + 1] = total[:, depth:].astype(BF)

    def activate(g, u):
        return (g / (1.0 + jnp.exp(-g)) * u).astype(BF)

    def pipeline(m):
        last = m == halves - 1
        own_rows[m].wait()
        yield from gather_line(m, lambda i: tokens.at[m, i])
        if m == 0:
            for copy in loads["gu1"]:
                copy.wait()
        gate_up(m, tokens)
        at = lambda i: part.at[m, piece(i)]
        yield from scatter_narrow(m, at, near.at[m], across.at[m])
        if last:
            loads["gu2"] = [load(0, g2, wgu.at[0]), load(1, u2, wgu.at[1])]
        g, u = (
            part[m, piece(n), s].astype(F32)
            + near[m, chip, :, s].astype(F32)
            + across[m, :, s].astype(F32)
            for s in (slice(0, units), slice(units, 2 * units))
        )
        hid1[m, piece(n)] = activate(g, u)
        yield from gather_narrow(m, lambda i: hid1.at[m, piece(i)])
        if m == 0:
            loads["d1"][0].wait()
        down(m, hid1)
        if last:
            loads["d2"] = [load(2, d2, wd)]
        yield from scatter_line(m, lambda i: dpart.at[m, i], zr.at[m], zl.at[m])
        acc_h[...] = tokens[m, z].astype(F32) + dpart[m, z].astype(F32)

        @pl.when(z >= 1)
        def _():
            acc_h[...] += zr[m, LINE - 2].astype(F32)

        @pl.when(z < LINE - 1)
        def _():
            acc_h[...] += zl[m, LINE - 2].astype(F32)

        mid[m, n] = acc_h[...].astype(BF)
        yield from gather_narrow(m, lambda i: mid.at[m, i])
        if m == 0:
            for copy in loads["gu2"]:
                copy.wait()
        flush(m)
        gate_up(m, mid)
        yield from scatter_line(m, at, yr.at[m], yl.at[m])
        acc_gu[...] = part[m, piece(z)].astype(F32)

        @pl.when(z >= 1)
        def _():
            acc_gu[...] += yr[m, LINE - 2].astype(F32)

        @pl.when(z < LINE - 1)
        def _():
            acc_gu[...] += yl[m, LINE - 2].astype(F32)

        hid2[m, piece(z)] = activate(acc_gu[:, :units], acc_gu[:, units:])
        yield from gather_line(m, lambda i: hid2.at[m, piece(i)])
        if m == 0:
            loads["d2"][0].wait()
        down(m, hid2)
        yield from scatter_narrow(m, lambda i: dpart.at[m, i], near8.at[m], across8.at[m])
        out[pl.ds(m * rows, rows)] = (
            mid[m, n].astype(F32) + dpart[m, n].astype(F32)
            + near8[m, chip].astype(F32) + across8[m].astype(F32)
        ).astype(BF)
        flush(m)

    runs = [pipeline(m) for m in range(halves)]
    alive = [True] * halves
    turn = 0
    while any(alive):
        for m in range(halves):
            if alive[m] and turn >= m * LAG:
                try:
                    next(runs[m])
                except StopIteration:
                    alive[m] = False
        turn += 1


N_MESSAGES = 2 * 36


def fused(tokens, gate_one, up_one, down_one, gate_two, up_two, down_two):
    m, rows, depth = 2, tokens.shape[0] // 2, tokens.shape[1]
    width, units = gate_one.shape
    quarter = rows // LINE
    vmem = pltpu.VMEM
    scratch = [
        vmem((2, width, units), BF),
        vmem((units, width), BF),
        vmem((m, LINE, rows, depth), BF),
        vmem((m, rows, 2 * units), BF),
        vmem((m, 2, quarter, 2 * units), BF),
        vmem((m, quarter, 2 * units), BF),
        vmem((m, rows, units), BF),
        vmem((m, LINE, rows, depth), BF),
        vmem((m, LINE - 1, rows, depth), BF),
        vmem((m, LINE - 1, rows, depth), BF),
        vmem((m, LINE, rows, depth), BF),
        vmem((m, LINE - 1, quarter, 2 * units), BF),
        vmem((m, LINE - 1, quarter, 2 * units), BF),
        vmem((m, rows, units), BF),
        vmem((m, 2, rows, depth), BF),
        vmem((m, rows, depth), BF),
        vmem((quarter, 2 * units), F32),
        vmem((rows, depth), F32),
        pltpu.SemaphoreType.DMA((3,)),
        pltpu.SemaphoreType.DMA((2,)),
        pltpu.SemaphoreType.DMA((N_MESSAGES,)),
        pltpu.SemaphoreType.DMA((N_MESSAGES,)),
    ]
    flops = 2 * tokens.shape[0] * width * units * 6
    return pl.pallas_call(
        kernel,
        out_shape=jax.ShapeDtypeStruct(tokens.shape, BF),
        in_specs=[pl.BlockSpec(memory_space=pl.ANY)] * 7,
        out_specs=pl.BlockSpec(memory_space=pltpu.VMEM),
        scratch_shapes=scratch,
        compiler_params=pltpu.CompilerParams(
            collective_id=0, has_side_effects=True, vmem_limit_bytes=60 * MIB
        ),
        cost_estimate=pl.CostEstimate(
            flops=flops, bytes_accessed=12 * width * units, transcendentals=0
        ),
    )(
        tokens, gate_one, up_one, down_one,
        gate_two.reshape(-1, gate_two.shape[2]),
        up_two.reshape(-1, up_two.shape[2]),
        down_two.reshape(down_two.shape[0], -1),
    )


def fits(mesh, tokens, gate_one, up_one, down_one, gate_two, up_two, down_two):
    rows, depth = tokens.shape
    width, units = gate_one.shape
    return (
        mesh.shape["wide"] == LINE and mesh.shape["narrow"] == LINE
        and rows % (32 * LINE) == 0 and units % 256 == 0 and depth % 64 == 0
        and width == LINE * depth and gate_two.shape[:2] == (LINE, depth)
        and 12 * width * units < 50 * MIB
    )


def solution(mesh):
    def per_device(*arrays):
        return (fused if fits(mesh, *arrays) else plain)(*arrays)

    return jax.shard_map(
        per_device,
        mesh=mesh,
        in_specs=(
            P("groups", ("narrow", "wide")),
            P("narrow", "wide"),
            P("narrow", "wide"),
            P("wide", "narrow"),
            P(None, "wide", "narrow"),
            P(None, "wide", "narrow"),
            P("narrow", None, "wide"),
        ),
        out_specs=P("groups", ("narrow", "wide")),
        check_vma=False,
    )
```

time: 437 us -> 244 us (0.56)
  waiting for transfers between devices: 350 us -> 0 us
  Pallas kernels: 0 us -> 228 us
  matrix products: 61.7 us -> 0 us
  between operations: 13.5 us -> 0.01 us
  local copies, waits for them, and re-layouts: 2.64 us -> 15.6 us
  other arithmetic: 8.67 us -> 0 us
    pallas_call x0 -> x1, Pallas kernels: none -> 228 us  [fused(): pl.pallas_call(kernel, out_shape=jax.ShapeDtypeStruct(tokens.shape, BF),...]
    reduce_scatter x6 -> x0, waiting for transfers between devices: 209 us -> none  [the longest x1 49.9 us: per_device(): lax.psum_scatter(gate_part2.astype(jnp.bfloat16), 'wide', scatter_dimensi...]
    all_gather x4 -> x0, waiting for transfers between devices: 140 us -> none  [the longest x1 50.1 us: per_device(): lax.all_gather(hidden_share2, 'wide', axis=1, tiled=True)]
    dot_general x6 -> x0, matrix products: 61.7 us -> none  [the longest x2 22.5 us: pair_fold(): jnp.dot(piece, first_matrix, preferred_element_type=jnp.float32)]
    reshape x0 -> x1, local copies, waits for them, and re-layouts: none -> 11.5 us  [fused(): down_two.reshape(down_two.shape[0], -1)]
    convert_element_type x4 -> x0, other arithmetic: 8.67 us -> none  [the longest x2 4.87 us: swiglu(): return (jax.nn.silu(gate) * up_value).astype(jnp.bfloat16)]
  transfers between devices with their start and end apart: 10 -> 0, of which waited for: 10 -> 0; matrix products, arithmetic and copies ran while one was open for 5% -> 0% of each run, Pallas kernels for 0% -> 0%
where the time goes in v1:
time: 244 us
  Pallas kernels  228 us (93%)
  local copies, waits for them, and re-layouts  15.6 us (6%)
    pallas_call x1, Pallas kernels, fused(): pl.pallas_call(kernel, out_shape=jax.ShapeDtypeStruct(tokens.shape, BF),...  228 us
    reshape x1, local copies, waits for them, and re-layouts, fused(): down_two.reshape(down_two.shape[0], -1)  11.5 us

profile of v1, /device:TPU:0, one launch (start us, length us, event | category | flops | bytes accessed | tf_op | source)
XLA Modules:
  0.0 243.6 jit_solution(2881025921932241781)
XLA Ops:
  0.0 2.1 copy.11.tok
  2.1 11.5 %copy.12.d2 = bf16[2304,1792]{1,0:T(8,128)(2,1)} copy(bf16[2304,1792]{0,1:T(8,128)(2,1)} %bitcast.3) | data formatting | bytes 16515072 | tf_op jit(solution)/shard_map/reshape | solution.py:373
  13.6 228.0 %shard_map.73 = bf16[512,448]{1,0:T(8,128)(2,1)} custom-call(bf16[512,448]{1,0:T(8,128)(2,1)} %copy.11.tok, bf16[1792,2304]{1,0:T(8,128)(2,1)} %g1.1, bf16[1792,2304]{1,0:T(8,128)(2,1)} %u1_.1, bf16[2304,1792]{1,0:T(8,128)(2,1)} %d1.1, bf16[1792,2304]{1,0:T(8,128)(2,1)} %bitcast.4, bf16[1792,2304]{1,0:T(8,128)(2,1)} %bitcast.5, bf16[2304,1792]{1,0:T(8,128)(2,1)} %copy.12.d2), custom_call_target="tpu_custom_call" | custom-call | flops 25367150592 | bytes 49545216 | tf_op jit(solution)/shard_map/pallas_call | solution.py:357
  241.6 2.0 copy.13
